TPU v7x, 256 devices: a whole 4x4x8 slice. The times are simulated.
256 devices in a mesh: grp: 16 (over y, x_hi, core), sh: 16 (over z, x_lo).
Axes of the slice: x: 4 (x_hi: 2, x_lo: 2; x = x_hi * 2 + x_lo), y: 4, z: 8, core: 2. Of those that a mesh axis runs over, the one named last changes fastest.
Arguments:
- factors: bfloat16 [48, 128, 14336], P('grp', None, 'sh'), may hold values from -0.5 to 0.5
- screen: int32 [48, 1, 112], P('grp', None, 'sh'), may hold values 0 or 1
- occ_energy: float32 [48], replicated, may hold values from -1.5 to -0.3
- virt_energy: float32 [128], replicated, may hold values from 0.5 to 3
Outputs:
- gamma: bfloat16 [48, 128, 14336], P('grp', 'sh')
Inputs may be any that keep to these rules, and one draw needn't show every extreme that they name: `screen`: 1 keeps a block of 128 virtual by 128 auxiliary functions of one occupied orbital, 0 screens it out.
All inputs are finite; a program needn't handle non-finite values.
Results may differ from a plain program's by a relative error of at most 0.0049.
Values may be sent and summed in bfloat16 or wider, within the bound.
No kernel may reach another device: no remote copies, remote signals or barrier semaphores. Data moves between devices by JAX's collectives and lax.ppermute only.
A program may use at most 64 MiB of HBM per device.

v0:
```python
import functools

import jax
import jax.numpy as jnp
from jax import lax
from jax.experimental import pallas as pl
from jax.experimental.pallas import tpu as pltpu
from jax.sharding import Mesh, PartitionSpec as P

BLK = 128
NY, NXH, NC, NZ, NXL = 4, 2, 2, 8, 2
GRP = ("y", "xh", "core")
SH = ("z", "xl")
X = ("xh", "xl")
BF = jnp.bfloat16
F32 = jnp.float32


def flip_x(value, bits):
    return lax.ppermute(value, X, [(i, i ^ bits) for i in range(NXH * NXL)])


def shift(value, axis, steps):
    count = lax.axis_size(axis)
    return lax.ppermute(value, axis, [(i, (i + steps) % count) for i in range(count)])


def flip_core(value):
    return lax.ppermute(value, "core", [(0, 1), (1, 0)])


def dot_t(a, b):
    return lax.dot_general(a, b, (((1,), (1,)), ((), ())), preferred_element_type=F32)


def coulomb_kernel(own, xlf, bof, xh, *refs):
    near, far, (out, send_up, send_down, stack, left) = refs[0:4], refs[4:8], refs[8:13]
    z, xl, c = lax.axis_index("z"), lax.axis_index("xl"), lax.axis_index("core")
    rows, half = own.shape

    def lay(mine, flipped, at):
        here, there = slice(at * half, (at + 1) * half), slice((1 - at) * half, (2 - at) * half)
        left[0:rows, here] = mine[...]
        left[0:rows, there] = flipped[...]
        left[rows:, here] = xh[...]
        left[rows:, there] = bof[...]

    @pl.when(xl == c)
    def _():
        lay(own, far[0], 0)

    @pl.when(xl != c)
    def _():
        lay(own, xlf, 1)

    for d in range(NY):
        for k, pieces in enumerate((near, far)):
            stack[d * rows:(d + 1) * rows, k * half:(k + 1) * half] = pieces[d][...]
    for pair in range(NY // 2):
        got = dot_t(left[...], stack[pair * 2 * rows:(pair + 1) * 2 * rows, :])
        for e in range(2):
            for dd in range(2):
                at = lax.rem(e * NY + pair * 2 + dd + NZ - z, NZ)
                out[at] = got[e * rows:(e + 1) * rows, dd * rows:(dd + 1) * rows]
    send_up[...] = out[NZ // 2, 0:rows // 2, :].astype(BF)
    send_down[...] = out[NZ // 2, rows // 2:rows, :].astype(BF)


def combined_kernel(occ_ref, v_col, v_row, mine, up, down, out, scr):
    y, xh, c, z, xl = (lax.axis_index(n) for n in ("y", "xh", "core", "z", "xl"))
    virt = v_row.shape[1]
    count = mine.shape[0] // virt
    e, d = z // NY, lax.rem(z, NY)
    row_occ = ((y * NXH + lax.rem(xh + e, NXH)) * NC + c) * count
    col_occ = ((lax.rem(y + NY - d, NY) * NXH + xh) * NC + xl) * count
    for i in range(count):
        for j in range(count):
            tile = (pl.ds(i * virt, virt), pl.ds(j * virt, virt))
            total = mine[tile] + up[tile].astype(F32) + down[tile].astype(F32)
            row, col = v_col[...] - occ_ref[row_occ + i], v_row[...] - occ_ref[col_occ + j]
            amp = (total / (row + col)).astype(BF).astype(F32)
            comb = 2.0 * amp - amp.T
            for zp in range(NZ):
                for h in range(NXL):
                    at = (zp * NXL + h) * 8
                    scr[h, (zp * count + i) * 8:(zp * count + i + 1) * 8, j * virt:(j + 1) * virt] = comb[at:at + 8]
    for h in range(NXL):
        out[h] = scr[h].astype(BF)


def gamma_kernel(*refs, group):
    combs, stack, outs, (left, scr) = refs[0:9], refs[9], refs[10:-2], refs[-2:]
    half, rows = combs[0].shape[1:]
    z, xl = lax.axis_index("z"), lax.axis_index("xl")
    part = combs[7].shape[1]
    places = [(ref, step, 0) for ref, step in zip(combs[:7], (0, 1, -1, 2, -2, 3, -3))]
    for ref, step, row0 in places + [(combs[7], 4, 0), (combs[8], 4, part)]:
        source = lax.rem(z + NZ - step, NZ)

        @pl.when(source // NY == group)
        def _(ref=ref, source=source, row0=row0):
            cols = pl.ds(pl.multiple_of(lax.rem(source, NY) * rows, 128), rows)
            for fl in range(2):
                at = fl * half + row0
                left[at:at + ref.shape[1], cols] = ref[lax.rem(xl + fl, 2)]

    width = stack.shape[1] // 2
    piece = half // NZ
    for k in range(2):
        cols = slice(k * width, (k + 1) * width)
        acc = jnp.dot(left[...], stack[:, cols], preferred_element_type=F32)
        for zp in range(NZ):
            at = lax.rem(zp + NZ - z, NZ)
            scr[0, at, :, cols] = acc[zp * piece:(zp + 1) * piece]
            scr[1, at, :, cols] = acc[half + zp * piece:half + (zp + 1) * piece]
    n = NZ // 2
    for fl in range(2):
        for p in range(2):
            outs[2 * fl + p][...] = scr[fl, p * n:(p + 1) * n].astype(outs[2 * fl + p].dtype)


def assemble_kernel(*refs):
    out = refs[-1]
    z, core = lax.axis_index("z"), lax.axis_index("core")
    half = refs[0].shape[1] // 2
    for k in range(NZ):
        source = lax.rem(z + NZ - k, NZ)
        for part in range(2):
            start = pl.multiple_of(source * 2 * half + lax.rem(core + part, 2) * half, 128)
            out[:, pl.ds(start, half)] = refs[k][:, part * half:(part + 1) * half]


def on_device(factors, screen, occ_energy, virt_energy):
    occ_g, virt, aux = factors.shape
    rows = occ_g * virt
    hr = rows // 2
    wide_mask = jnp.repeat(jnp.repeat(screen, BLK, axis=1), BLK, axis=2)
    own = (factors * wide_mask.astype(BF)).reshape(rows, aux)

    with jax.named_scope("gather"):
        j0 = lax.ppermute(own, ("core", "xl"), [(0, 0), (1, 2), (2, 1), (3, 3)])
        bof = flip_x(own, 3)
        xh = flip_x(own, 2)
        f0 = flip_core(j0)
        j1, j2, j3 = (shift(j0, "y", d) for d in (1, 2, 3))
        own_b, f0, bof, xh = lax.optimization_barrier((own, f0, bof, xh))
        xlf = lax.ppermute(own_b, ("core", "xl"), [(0, 1), (3, 2)])
        j1, j3, xlf = lax.optimization_barrier((j1, j3, xlf))
        near = [j0, j1, j2, j3]
        far = [f0] + [flip_core(p) for p in near[1:]]

    vmem = pl.BlockSpec(memory_space=pltpu.VMEM)
    smem = pl.BlockSpec(memory_space=pltpu.SMEM)
    params = pltpu.CompilerParams(vmem_limit_bytes=48 << 20)

    with jax.named_scope("coulomb"):
        parts, up, down, stack = pl.pallas_call(
            coulomb_kernel,
            out_shape=[
                jax.ShapeDtypeStruct((NZ, rows, rows), F32),
                jax.ShapeDtypeStruct((hr, rows), BF),
                jax.ShapeDtypeStruct((hr, rows), BF),
                jax.ShapeDtypeStruct((NY * rows, 2 * aux), BF),
            ],
            in_specs=[vmem] * 12,
            out_specs=[vmem] * 4,
            scratch_shapes=[pltpu.VMEM((2 * rows, 2 * aux), BF)],
            compiler_params=params,
        )(own, xlf, bof, xh, *near, *far)

    with jax.named_scope("ring"):
        up, down = shift(up, "z", 1), shift(down, "z", -1)
        up = jnp.concatenate([up.astype(F32) + parts[3, :hr], parts[3, hr:]])
        down = jnp.concatenate([parts[5, :hr], down.astype(F32) + parts[5, hr:]])
        for k in (2, 1, 0):
            up, down = shift(up.astype(BF), "z", 1), shift(down.astype(BF), "z", -1)
            if k:
                up, down = up.astype(F32) + parts[k], down.astype(F32) + parts[NZ - k]

    with jax.named_scope("combined"):
        comb = pl.pallas_call(
            combined_kernel,
            out_shape=jax.ShapeDtypeStruct((NXL, hr, rows), BF),
            in_specs=[smem] + [vmem] * 5,
            out_specs=vmem,
            scratch_shapes=[pltpu.VMEM((NXL, hr, rows), F32)],
            compiler_params=params,
        )(occ_energy, virt_energy[:, None], virt_energy[None, :], parts[0], up, down)
        up1, down1 = shift(comb, "z", 1), shift(comb, "z", -1)
        up2, down2 = shift(up1, "z", 1), shift(down1, "z", -1)
        up3, down3 = shift(up2, "z", 1), shift(down2, "z", -1)
        up4, down4 = shift(up3[:, :hr // 2], "z", 1), shift(down3[:, hr // 2:], "z", -1)
        combs = [comb, up1, down1, up2, down2, up3, down3, up4, down4]

    with jax.named_scope("gamma"):
        piece = hr // NZ

        def gamma_of(group, types):
            return pl.pallas_call(
                functools.partial(gamma_kernel, group=group),
                out_shape=[jax.ShapeDtypeStruct((NZ // 2, piece, 2 * aux), t) for t in types],
                in_specs=[vmem] * 10,
                out_specs=[vmem] * 4,
                scratch_shapes=[
                    pltpu.VMEM((2 * hr, NY * rows), BF),
                    pltpu.VMEM((2, NZ, piece, 2 * aux), F32),
                ],
                compiler_params=params,
            )(*combs, stack)

        to_xh0, to_xh1, to_both0, to_both1 = gamma_of(1, (BF, BF, F32, F32))
        via_both, via_xl = flip_x(to_xh0, 3), flip_x(to_xh1, 1)
        mine0, mine1, to_xl0, to_xl1 = gamma_of(0, (F32, F32, F32, F32))
        to_both = jnp.concatenate([to_both0, to_both1 + via_xl.astype(F32)]).astype(BF)
        to_xl = jnp.concatenate([to_xl0 + via_both.astype(F32), to_xl1]).astype(BF)
        mine = jnp.concatenate([mine0, mine1])
        from_both, from_xl = flip_x(to_both, 3), flip_x(to_xl, 1)
        total = (mine + from_xl.astype(F32) + from_both.astype(F32)).astype(BF)

    with jax.named_scope("spread"):
        got = [total[0]] + [shift(total[k], "z", k) for k in range(1, NZ)]
        out = pl.pallas_call(
            assemble_kernel,
            out_shape=jax.ShapeDtypeStruct((piece, NZ * 2 * aux), BF),
            in_specs=[vmem] * NZ,
            out_specs=vmem,
            compiler_params=pltpu.CompilerParams(vmem_limit_bytes=16 << 20),
        )(*got)
    return out.reshape(occ_g, piece // occ_g, NZ * 2 * aux)


def solution(mesh):
    split = Mesh(mesh.devices.reshape(NY, NXH, NC, NZ, NXL), ("y", "xh", "core", "z", "xl"))
    placed = (P(GRP, None, SH), P(GRP, None, SH), P(), P())
    return jax.shard_map(on_device, mesh=split, in_specs=placed, out_specs=P(GRP, SH, None), check_vma=False)
```

profile of v0, /device:TPU:32, one launch (start us, length us, event | category | flops | bytes accessed | tf_op | source)
XLA Modules:
  0.0 202.4 jit_solution(15701196632681993013)
XLA Ops:
  2.7 4.3 %collective-permute-start.4 = (bf16[384,896]{1,0:T(8,128)(2,1)S(1)}, bf16[384,896]{1,0:T(8,128)(2,1)S(1)}, u32[]{:S(2)}, u32[]{:S(2)}) collective-permute-start(bf16[384,896]{1,0:T(8,128)(2,1)S(1)} %bitcast.59), channel_id=1, source_target_pairs={{0,33},{1,32},{32,1},{33,0},{2,35},{3,34},{34,3},{35,2},{4,37},{5,... | collective-permute-start | bytes 2064392 | tf_op jit(solution)/shard_map/gather/ppermute | solution.py:20
  7.5 11.1 %collective-permute-start.3 = (bf16[384,896]{1,0:T(8,128)(2,1)S(1)}, bf16[384,896]{1,0:T(8,128)(2,1)S(1)}, u32[]{:S(2)}, u32[]{:S(2)}) collective-permute-start(bf16[384,896]{1,0:T(8,128)(2,1)S(1)} %collective-permute-done.refs_0_), channel_id=1, source_target_pairs={{0,16},{16,0},{1,17},{17,1},{2,18},{18,2},{3,19},{19,3},{4,20},{20... | collective-permute-start | bytes 2064392 | tf_op jit(solution)/shard_map/gather/ppermute | solution.py:29
  21.9 15.3 %collective-permute-done.4.bof = bf16[384,896]{1,0:T(8,128)(2,1)S(1)} collective-permute-done((bf16[384,896]{1,0:T(8,128)(2,1)S(1)}, bf16[384,896]{1,0:T(8,128)(2,1)S(1)}, u32[]{:S(2)}, u32[]{:S(2)}) %collective-permute-start.4) | collective-permute-done | bytes 688160 | tf_op jit(solution)/shard_map/gather/ppermute | solution.py:20
  37.2 3.2 %collective-permute-start.7 = (bf16[384,896]{1,0:T(8,128)(2,1)S(1)}, bf16[384,896]{1,0:T(8,128)(2,1)S(1)}, u32[]{:S(2)}, u32[]{:S(2)}) collective-permute-start(bf16[384,896]{1,0:T(8,128)(2,1)S(1)} %collective-permute-done.refs_0_), channel_id=1, source_target_pairs={{0,128},{64,192},{128,0},{192,64},{1,129},{65,193},{129,1},{193,65... | collective-permute-start | bytes 2064392 | tf_op jit(solution)/shard_map/gather/ppermute | solution.py:25
  40.4 3.2 %collective-permute-start.6 = (bf16[384,896]{1,0:T(8,128)(2,1)S(1)}, bf16[384,896]{1,0:T(8,128)(2,1)S(1)}, u32[]{:S(2)}, u32[]{:S(2)}) collective-permute-start(bf16[384,896]{1,0:T(8,128)(2,1)S(1)} %bitcast.61), channel_id=1, source_target_pairs={{0,1},{17,16},{2,3},{19,18},{4,5},{21,20},{6,7},{23,22},{8,9},{25,... | collective-permute-start | bytes 2064392 | tf_op jit(solution)/shard_map/gather/ppermute | solution.py:147
  43.6 13.1 %collective-permute-done.7.refs_2_ = bf16[384,896]{1,0:T(8,128)(2,1)S(1)} collective-permute-done((bf16[384,896]{1,0:T(8,128)(2,1)S(1)}, bf16[384,896]{1,0:T(8,128)(2,1)S(1)}, u32[]{:S(2)}, u32[]{:S(2)}) %collective-permute-start.7) | collective-permute-done | bytes 688160 | tf_op jit(solution)/shard_map/gather/ppermute | solution.py:25
  61.7 10.2 %coulomb.1 = (f32[8,384,384]{2,1,0:T(8,128)}, bf16[192,384]{1,0:T(8,128)(2,1)S(1)}, bf16[192,384]{1,0:T(8,128)(2,1)S(1)}, bf16[1536,1792]{1,0:T(8,128)(2,1)}) custom-call(bf16[384,896]{1,0:T(8,128)(2,1)S(1)} %bitcast.62, bf16[384,896]{1,0:T(8,128)(2,1)S(1)} %collective-permute-done.6.xlf, bf16[384,896]{1,0:T(8,128)(2,1)S(1)} %collective-permute-done.4.bof, ...), custom_call_target="tpu_custom_call" | custom-call | tf_op jit(solution)/shard_map/coulomb/pallas_call | solution.py:157
  76.7 3.8 %collective-permute-done.11 = bf16[192,384]{1,0:T(8,128)(2,1)S(1)} collective-permute-done((bf16[192,384]{1,0:T(8,128)(2,1)S(1)}, bf16[192,384]{1,0:T(8,128)(2,1)S(1)}, u32[]{:S(2)}, u32[]{:S(2)}) %collective-permute-start.11) | collective-permute-done | bytes 147488 | tf_op jit(solution)/shard_map/ring/ppermute | solution.py:25
  82.5 3.4 %collective-permute-start.12 = (bf16[384,384]{1,0:T(8,128)(2,1)S(1)}, bf16[384,384]{1,0:T(8,128)(2,1)S(1)}, u32[]{:S(2)}, u32[]{:S(2)}) collective-permute-start(bf16[384,384]{1,0:T(8,128)(2,1)S(1)} %pad_maximum_fusion.2), channel_id=1, source_target_pairs={{0,2},{2,4},{4,6},{6,8},{8,10},{10,12},{12,14},{14,0},{1,3},{3,5},... | collective-permute-start | bytes 884744 | tf_op jit(solution)/shard_map/ring/ppermute | solution.py:25
  86.0 5.9 %collective-permute-done.12 = bf16[384,384]{1,0:T(8,128)(2,1)S(1)} collective-permute-done((bf16[384,384]{1,0:T(8,128)(2,1)S(1)}, bf16[384,384]{1,0:T(8,128)(2,1)S(1)}, u32[]{:S(2)}, u32[]{:S(2)}) %collective-permute-start.12) | collective-permute-done | bytes 294944 | tf_op jit(solution)/shard_map/ring/ppermute | solution.py:25
  97.1 5.0 %collective-permute-done.13 = bf16[384,384]{1,0:T(8,128)(2,1)S(1)} collective-permute-done((bf16[384,384]{1,0:T(8,128)(2,1)S(1)}, bf16[384,384]{1,0:T(8,128)(2,1)S(1)}, u32[]{:S(2)}, u32[]{:S(2)}) %collective-permute-start.13) | collective-permute-done | bytes 294944 | tf_op jit(solution)/shard_map/ring/ppermute | solution.py:25
  107.1 3.5 %collective-permute-done.14.up = bf16[384,384]{1,0:T(8,128)(2,1)S(1)} collective-permute-done((bf16[384,384]{1,0:T(8,128)(2,1)S(1)}, bf16[384,384]{1,0:T(8,128)(2,1)S(1)}, u32[]{:S(2)}, u32[]{:S(2)}) %collective-permute-start.14) | collective-permute-done | bytes 294944 | tf_op jit(solution)/shard_map/ring/ppermute | solution.py:25
  115.5 7.3 %collective-permute-done.19.refs_1_ = bf16[2,192,384]{2,1,0:T(8,128)(2,1)S(1)} collective-permute-done((bf16[2,192,384]{2,1,0:T(8,128)(2,1)S(1)}, bf16[2,192,384]{2,1,0:T(8,128)(2,1)S(1)}, u32[]{:S(2)}, u32[]{:S(2)}) %collective-permute-start.19) | collective-permute-done | bytes 294944 | tf_op jit(solution)/shard_map/combined/ppermute | solution.py:25
  125.1 7.3 %collective-permute-done.21.refs_3_ = bf16[2,192,384]{2,1,0:T(8,128)(2,1)S(1)} collective-permute-done((bf16[2,192,384]{2,1,0:T(8,128)(2,1)S(1)}, bf16[2,192,384]{2,1,0:T(8,128)(2,1)S(1)}, u32[]{:S(2)}, u32[]{:S(2)}) %collective-permute-start.21) | collective-permute-done | bytes 294944 | tf_op jit(solution)/shard_map/combined/ppermute | solution.py:25
  134.4 5.2 %collective-permute-done.23.refs_5_ = bf16[2,192,384]{2,1,0:T(8,128)(2,1)S(1)} collective-permute-done((bf16[2,192,384]{2,1,0:T(8,128)(2,1)S(1)}, bf16[2,192,384]{2,1,0:T(8,128)(2,1)S(1)}, u32[]{:S(2)}, u32[]{:S(2)}) %collective-permute-start.23) | collective-permute-done | bytes 294944 | tf_op jit(solution)/shard_map/combined/ppermute | solution.py:25
  146.7 5.8 %gamma.3 = (bf16[4,24,1792]{2,1,0:T(8,128)(2,1)S(1)}, bf16[4,24,1792]{2,1,0:T(8,128)(2,1)S(1)}, f32[4,24,1792]{2,1,0:T(8,128)S(1)}, f32[4,24,1792]{2,1,0:T(8,128)S(1)}) custom-call(bf16[2,192,384]{2,1,0:T(8,128)(2,1)S(1)} %combined.1.refs_0_, bf16[2,192,384]{2,1,0:T(8,128)(2,1)S(1)} %collective-permute-done.19.refs_1_, ...), custom_call_target="tpu_custom_call" | custom-call | tf_op jit(solution)/shard_map/gamma/pallas_call | solution.py:199
  152.6 5.6 %gamma.2 = (f32[4,24,1792]{2,1,0:T(8,128)S(1)}, f32[4,24,1792]{2,1,0:T(8,128)S(1)}, f32[4,24,1792]{2,1,0:T(8,128)S(1)}, f32[4,24,1792]{2,1,0:T(8,128)S(1)}) custom-call(bf16[2,192,384]{2,1,0:T(8,128)(2,1)S(1)} %combined.1.refs_0_, bf16[2,192,384]{2,1,0:T(8,128)(2,1)S(1)} %collective-permute-done.19.refs_1_, ...), custom_call_target="tpu_custom_call" | custom-call | tf_op jit(solution)/shard_map/gamma/pallas_call | solution.py:199
  161.6 5.8 %collective-permute-done.29 = bf16[4,24,1792]{2,1,0:T(8,128)(2,1)S(1)} collective-permute-done((bf16[4,24,1792]{2,1,0:T(8,128)(2,1)S(1)}, bf16[4,24,1792]{2,1,0:T(8,128)(2,1)S(1)}, u32[]{:S(2)}, u32[]{:S(2)}) %collective-permute-start.29) | collective-permute-done | bytes 344096 | tf_op jit(solution)/shard_map/gamma/ppermute | solution.py:20
  170.6 4.2 %collective-permute-done.28 = bf16[8,24,1792]{2,1,0:T(8,128)(2,1)S(1)} collective-permute-done((bf16[8,24,1792]{2,1,0:T(8,128)(2,1)S(1)}, bf16[8,24,1792]{2,1,0:T(8,128)(2,1)S(1)}, u32[]{:S(2)}, u32[]{:S(2)}) %collective-permute-start.28) | collective-permute-done | bytes 688160 | tf_op jit(solution)/shard_map/gamma/ppermute | solution.py:20
  174.8 5.0 %collective-permute-done.30 = bf16[8,24,1792]{2,1,0:T(8,128)(2,1)S(1)} collective-permute-done((bf16[8,24,1792]{2,1,0:T(8,128)(2,1)S(1)}, bf16[8,24,1792]{2,1,0:T(8,128)(2,1)S(1)}, u32[]{:S(2)}, u32[]{:S(2)}) %collective-permute-start.30) | collective-permute-done | bytes 688160 | tf_op jit(solution)/shard_map/gamma/ppermute | solution.py:20
  181.7 3.2 %collective-permute-start.32 = (bf16[24,1792]{1,0:T(8,128)(2,1)S(1)}, bf16[24,1792]{1,0:T(8,128)(2,1)S(1)}, u32[]{:S(2)}, u32[]{:S(2)}) collective-permute-start(bf16[24,1792]{1,0:T(8,128)(2,1)S(1)} %get-tuple-element.56), channel_id=1, source_target_pairs={{0,4},{2,6},{4,8},{6,10},{8,12},{10,14},{12,0},{14,2},{1,5},{3,7},... | collective-permute-start | bytes 258056 | tf_op jit(solution)/shard_map/spread/ppermute | solution.py:25
  184.9 3.2 %collective-permute-start.33 = (bf16[24,1792]{1,0:T(8,128)(2,1)S(1)}, bf16[24,1792]{1,0:T(8,128)(2,1)S(1)}, u32[]{:S(2)}, u32[]{:S(2)}) collective-permute-start(bf16[24,1792]{1,0:T(8,128)(2,1)S(1)} %get-tuple-element.55), channel_id=1, source_target_pairs={{0,6},{2,8},{4,10},{6,12},{8,14},{10,0},{12,2},{14,4},{1,7},{3,9},... | collective-permute-start | bytes 258056 | tf_op jit(solution)/shard_map/spread/ppermute | solution.py:25
  188.1 3.2 %collective-permute-start.34 = (bf16[24,1792]{1,0:T(8,128)(2,1)S(1)}, bf16[24,1792]{1,0:T(8,128)(2,1)S(1)}, u32[]{:S(2)}, u32[]{:S(2)}) collective-permute-start(bf16[24,1792]{1,0:T(8,128)(2,1)S(1)} %get-tuple-element.54), channel_id=1, source_target_pairs={{0,8},{2,10},{4,12},{6,14},{8,0},{10,2},{12,4},{14,6},{1,9},{3,11}... | collective-permute-start | bytes 258056 | tf_op jit(solution)/shard_map/spread/ppermute | solution.py:25
  195.4 3.4 %collective-permute-done.34.refs_4_ = bf16[24,1792]{1,0:T(8,128)(2,1)S(1)} collective-permute-done((bf16[24,1792]{1,0:T(8,128)(2,1)S(1)}, bf16[24,1792]{1,0:T(8,128)(2,1)S(1)}, u32[]{:S(2)}, u32[]{:S(2)}) %collective-permute-start.34) | collective-permute-done | bytes 86048 | tf_op jit(solution)/shard_map/spread/ppermute | solution.py:25
  (95 shorter events, 60.9 us)
Async XLA Ops:
  2.7 34.5 %collective-permute-start.4 = (bf16[384,896]{1,0:T(8,128)(2,1)S(1)}, bf16[384,896]{1,0:T(8,128)(2,1)S(1)}, u32[]{:S(2)}, u32[]{:S(2)}) collective-permute-start(bf16[384,896]{1,0:T(8,128)(2,1)S(1)} %bitcast.59), channel_id=1, source_target_pairs={{0,33},{1,32},{32,1},{33,0},{2,35},{3,34},{34,3},{35,2},{4,37},{5,... | collective-permute-start | bytes 2064392 | tf_op jit(solution)/shard_map/gather/ppermute | solution.py:20
  7.0 33.4 %collective-permute-start.5 = (bf16[384,896]{1,0:T(8,128)(2,1)S(1)}, bf16[384,896]{1,0:T(8,128)(2,1)S(1)}, u32[]{:S(2)}, u32[]{:S(2)}) collective-permute-start(bf16[384,896]{1,0:T(8,128)(2,1)S(1)} %bitcast.60), channel_id=1, source_target_pairs={{0,32},{1,33},{32,0},{33,1},{2,34},{3,35},{34,2},{35,3},{4,36},{5,... | collective-permute-start | bytes 2064392 | tf_op jit(solution)/shard_map/gather/ppermute | solution.py:20
  7.5 32.9 %collective-permute-start.3 = (bf16[384,896]{1,0:T(8,128)(2,1)S(1)}, bf16[384,896]{1,0:T(8,128)(2,1)S(1)}, u32[]{:S(2)}, u32[]{:S(2)}) collective-permute-start(bf16[384,896]{1,0:T(8,128)(2,1)S(1)} %collective-permute-done.refs_0_), channel_id=1, source_target_pairs={{0,16},{16,0},{1,17},{17,1},{2,18},{18,2},{3,19},{19,3},{4,20},{20... | collective-permute-start | bytes 2064392 | tf_op jit(solution)/shard_map/gather/ppermute | solution.py:29
  18.6 38.1 %collective-permute-start.1 = (bf16[384,896]{1,0:T(8,128)(2,1)S(1)}, bf16[384,896]{1,0:T(8,128)(2,1)S(1)}, u32[]{:S(2)}, u32[]{:S(2)}) collective-permute-start(bf16[384,896]{1,0:T(8,128)(2,1)S(1)} %collective-permute-done.refs_0_), channel_id=1, source_target_pairs={{0,64},{64,128},{128,192},{192,0},{1,65},{65,129},{129,193},{193,1... | collective-permute-start | bytes 2064392 | tf_op jit(solution)/shard_map/gather/ppermute | solution.py:25
  20.2 36.5 %collective-permute-start.2 = (bf16[384,896]{1,0:T(8,128)(2,1)S(1)}, bf16[384,896]{1,0:T(8,128)(2,1)S(1)}, u32[]{:S(2)}, u32[]{:S(2)}) collective-permute-start(bf16[384,896]{1,0:T(8,128)(2,1)S(1)} %collective-permute-done.refs_0_), channel_id=1, source_target_pairs={{0,192},{64,0},{128,64},{192,128},{1,193},{65,1},{129,65},{193,129... | collective-permute-start | bytes 2064392 | tf_op jit(solution)/shard_map/gather/ppermute | solution.py:25
  37.2 19.5 %collective-permute-start.7 = (bf16[384,896]{1,0:T(8,128)(2,1)S(1)}, bf16[384,896]{1,0:T(8,128)(2,1)S(1)}, u32[]{:S(2)}, u32[]{:S(2)}) collective-permute-start(bf16[384,896]{1,0:T(8,128)(2,1)S(1)} %collective-permute-done.refs_0_), channel_id=1, source_target_pairs={{0,128},{64,192},{128,0},{192,64},{1,129},{65,193},{129,1},{193,65... | collective-permute-start | bytes 2064392 | tf_op jit(solution)/shard_map/gather/ppermute | solution.py:25
  40.4 16.3 %collective-permute-start.6 = (bf16[384,896]{1,0:T(8,128)(2,1)S(1)}, bf16[384,896]{1,0:T(8,128)(2,1)S(1)}, u32[]{:S(2)}, u32[]{:S(2)}) collective-permute-start(bf16[384,896]{1,0:T(8,128)(2,1)S(1)} %bitcast.61), channel_id=1, source_target_pairs={{0,1},{17,16},{2,3},{19,18},{4,5},{21,20},{6,7},{23,22},{8,9},{25,... | collective-permute-start | bytes 2064392 | tf_op jit(solution)/shard_map/gather/ppermute | solution.py:147
  82.5 9.5 %collective-permute-start.12 = (bf16[384,384]{1,0:T(8,128)(2,1)S(1)}, bf16[384,384]{1,0:T(8,128)(2,1)S(1)}, u32[]{:S(2)}, u32[]{:S(2)}) collective-permute-start(bf16[384,384]{1,0:T(8,128)(2,1)S(1)} %pad_maximum_fusion.2), channel_id=1, source_target_pairs={{0,2},{2,4},{4,6},{6,8},{8,10},{10,12},{12,14},{14,0},{1,3},{3,5},... | collective-permute-start | bytes 884744 | tf_op jit(solution)/shard_map/ring/ppermute | solution.py:25
  86.0 8.9 %collective-permute-start.16 = (bf16[384,384]{1,0:T(8,128)(2,1)S(1)}, bf16[384,384]{1,0:T(8,128)(2,1)S(1)}, u32[]{:S(2)}, u32[]{:S(2)}) collective-permute-start(bf16[384,384]{1,0:T(8,128)(2,1)S(1)} %pad_maximum_fusion.3), channel_id=1, source_target_pairs={{0,14},{2,0},{4,2},{6,4},{8,6},{10,8},{12,10},{14,12},{1,15},{3,1}... | collective-permute-start | bytes 884744 | tf_op jit(solution)/shard_map/ring/ppermute | solution.py:25
  113.4 9.4 %collective-permute-start.19 = (bf16[2,192,384]{2,1,0:T(8,128)(2,1)S(1)}, bf16[2,192,384]{2,1,0:T(8,128)(2,1)S(1)}, u32[]{:S(2)}, u32[]{:S(2)}) collective-permute-start(bf16[2,192,384]{2,1,0:T(8,128)(2,1)S(1)} %combined.1.refs_0_), channel_id=1, source_target_pairs={{0,2},{2,4},{4,6},{6,8},{8,10},{10,12},{12,14},{14,0},{1,3},{3,5},... | collective-permute-start | bytes 884744 | tf_op jit(solution)/shard_map/combined/ppermute | solution.py:25
  115.1 9.6 %collective-permute-start.20 = (bf16[2,192,384]{2,1,0:T(8,128)(2,1)S(1)}, bf16[2,192,384]{2,1,0:T(8,128)(2,1)S(1)}, u32[]{:S(2)}, u32[]{:S(2)}) collective-permute-start(bf16[2,192,384]{2,1,0:T(8,128)(2,1)S(1)} %combined.1.refs_0_), channel_id=1, source_target_pairs={{0,14},{2,0},{4,2},{6,4},{8,6},{10,8},{12,10},{14,12},{1,15},{3,1}... | collective-permute-start | bytes 884744 | tf_op jit(solution)/shard_map/combined/ppermute | solution.py:25
  122.8 9.5 %collective-permute-start.21 = (bf16[2,192,384]{2,1,0:T(8,128)(2,1)S(1)}, bf16[2,192,384]{2,1,0:T(8,128)(2,1)S(1)}, u32[]{:S(2)}, u32[]{:S(2)}) collective-permute-start(bf16[2,192,384]{2,1,0:T(8,128)(2,1)S(1)} %collective-permute-done.19.refs_1_), channel_id=1, source_target_pairs={{0,2},{2,4},{4,6},{6,8},{8,10},{10,12},{12,14},{14,0},{1,3},{3,5},... | collective-permute-start | bytes 884744 | tf_op jit(solution)/shard_map/combined/ppermute | solution.py:25
  124.7 9.3 %collective-permute-start.22 = (bf16[2,192,384]{2,1,0:T(8,128)(2,1)S(1)}, bf16[2,192,384]{2,1,0:T(8,128)(2,1)S(1)}, u32[]{:S(2)}, u32[]{:S(2)}) collective-permute-start(bf16[2,192,384]{2,1,0:T(8,128)(2,1)S(1)} %collective-permute-done.20.refs_2_), channel_id=1, source_target_pairs={{0,14},{2,0},{4,2},{6,4},{8,6},{10,8},{12,10},{14,12},{1,15},{3,1}... | collective-permute-start | bytes 884744 | tf_op jit(solution)/shard_map/combined/ppermute | solution.py:25
  152.5 9.0 %collective-permute-start.27 = (bf16[4,24,1792]{2,1,0:T(8,128)(2,1)S(1)}, bf16[4,24,1792]{2,1,0:T(8,128)(2,1)S(1)}, u32[]{:S(2)}, u32[]{:S(2)}) collective-permute-start(bf16[4,24,1792]{2,1,0:T(8,128)(2,1)S(1)} %get-tuple-element.38), channel_id=1, source_target_pairs={{0,33},{1,32},{32,1},{33,0},{2,35},{3,34},{34,3},{35,2},{4,37},{5,... | collective-permute-start | bytes 1032200 | tf_op jit(solution)/shard_map/gamma/ppermute | solution.py:20
  158.2 9.2 %collective-permute-start.29 = (bf16[4,24,1792]{2,1,0:T(8,128)(2,1)S(1)}, bf16[4,24,1792]{2,1,0:T(8,128)(2,1)S(1)}, u32[]{:S(2)}, u32[]{:S(2)}) collective-permute-start(bf16[4,24,1792]{2,1,0:T(8,128)(2,1)S(1)} %get-tuple-element.42), channel_id=1, source_target_pairs={{0,1},{1,0},{32,33},{33,32},{2,3},{3,2},{34,35},{35,34},{4,5},{5,4... | collective-permute-start | bytes 1032200 | tf_op jit(solution)/shard_map/gamma/ppermute | solution.py:20
  161.5 13.3 %collective-permute-start.28 = (bf16[8,24,1792]{2,1,0:T(8,128)(2,1)S(1)}, bf16[8,24,1792]{2,1,0:T(8,128)(2,1)S(1)}, u32[]{:S(2)}, u32[]{:S(2)}) collective-permute-start(bf16[8,24,1792]{2,1,0:T(8,128)(2,1)S(1)} %pad_maximum_fusion), channel_id=1, source_target_pairs={{0,1},{1,0},{32,33},{33,32},{2,3},{3,2},{34,35},{35,34},{4,5},{5,4... | collective-permute-start | bytes 2064392 | tf_op jit(solution)/shard_map/gamma/ppermute | solution.py:20
  167.6 12.2 %collective-permute-start.30 = (bf16[8,24,1792]{2,1,0:T(8,128)(2,1)S(1)}, bf16[8,24,1792]{2,1,0:T(8,128)(2,1)S(1)}, u32[]{:S(2)}, u32[]{:S(2)}) collective-permute-start(bf16[8,24,1792]{2,1,0:T(8,128)(2,1)S(1)} %pad_maximum_fusion.1), channel_id=1, source_target_pairs={{0,33},{1,32},{32,1},{33,0},{2,35},{3,34},{34,3},{35,2},{4,37},{5,... | collective-permute-start | bytes 2064392 | tf_op jit(solution)/shard_map/gamma/ppermute | solution.py:20
  180.1 12.5 %collective-permute-start.31 = (bf16[24,1792]{1,0:T(8,128)(2,1)S(1)}, bf16[24,1792]{1,0:T(8,128)(2,1)S(1)}, u32[]{:S(2)}, u32[]{:S(2)}) collective-permute-start(bf16[24,1792]{1,0:T(8,128)(2,1)S(1)} %get-tuple-element.57), channel_id=1, source_target_pairs={{0,2},{2,4},{4,6},{6,8},{8,10},{10,12},{12,14},{14,0},{1,3},{3,5},... | collective-permute-start | bytes 258056 | tf_op jit(solution)/shard_map/spread/ppermute | solution.py:25
  181.7 11.1 %collective-permute-start.32 = (bf16[24,1792]{1,0:T(8,128)(2,1)S(1)}, bf16[24,1792]{1,0:T(8,128)(2,1)S(1)}, u32[]{:S(2)}, u32[]{:S(2)}) collective-permute-start(bf16[24,1792]{1,0:T(8,128)(2,1)S(1)} %get-tuple-element.56), channel_id=1, source_target_pairs={{0,4},{2,6},{4,8},{6,10},{8,12},{10,14},{12,0},{14,2},{1,5},{3,7},... | collective-permute-start | bytes 258056 | tf_op jit(solution)/shard_map/spread/ppermute | solution.py:25
  184.9 10.6 %collective-permute-start.33 = (bf16[24,1792]{1,0:T(8,128)(2,1)S(1)}, bf16[24,1792]{1,0:T(8,128)(2,1)S(1)}, u32[]{:S(2)}, u32[]{:S(2)}) collective-permute-start(bf16[24,1792]{1,0:T(8,128)(2,1)S(1)} %get-tuple-element.55), channel_id=1, source_target_pairs={{0,6},{2,8},{4,10},{6,12},{8,14},{10,0},{12,2},{14,4},{1,7},{3,9},... | collective-permute-start | bytes 258056 | tf_op jit(solution)/shard_map/spread/ppermute | solution.py:25
  188.1 10.8 %collective-permute-start.34 = (bf16[24,1792]{1,0:T(8,128)(2,1)S(1)}, bf16[24,1792]{1,0:T(8,128)(2,1)S(1)}, u32[]{:S(2)}, u32[]{:S(2)}) collective-permute-start(bf16[24,1792]{1,0:T(8,128)(2,1)S(1)} %get-tuple-element.54), channel_id=1, source_target_pairs={{0,8},{2,10},{4,12},{6,14},{8,0},{10,2},{12,4},{14,6},{1,9},{3,11}... | collective-permute-start | bytes 258056 | tf_op jit(solution)/shard_map/spread/ppermute | solution.py:25
  191.3 10.2 %collective-permute-start.35 = (bf16[24,1792]{1,0:T(8,128)(2,1)S(1)}, bf16[24,1792]{1,0:T(8,128)(2,1)S(1)}, u32[]{:S(2)}, u32[]{:S(2)}) collective-permute-start(bf16[24,1792]{1,0:T(8,128)(2,1)S(1)} %get-tuple-element.53), channel_id=1, source_target_pairs={{0,10},{2,12},{4,14},{6,0},{8,2},{10,4},{12,6},{14,8},{1,11},{3,13... | collective-permute-start | bytes 258056 | tf_op jit(solution)/shard_map/spread/ppermute | solution.py:25
  192.7 8.8 %collective-permute-start.36 = (bf16[24,1792]{1,0:T(8,128)(2,1)S(1)}, bf16[24,1792]{1,0:T(8,128)(2,1)S(1)}, u32[]{:S(2)}, u32[]{:S(2)}) collective-permute-start(bf16[24,1792]{1,0:T(8,128)(2,1)S(1)} %get-tuple-element.52), channel_id=1, source_target_pairs={{0,12},{2,14},{4,0},{6,2},{8,4},{10,6},{12,8},{14,10},{1,13},{3,15... | collective-permute-start | bytes 258056 | tf_op jit(solution)/shard_map/spread/ppermute | solution.py:25
  192.8 8.7 %collective-permute-start.37 = (bf16[24,1792]{1,0:T(8,128)(2,1)S(1)}, bf16[24,1792]{1,0:T(8,128)(2,1)S(1)}, u32[]{:S(2)}, u32[]{:S(2)}) collective-permute-start(bf16[24,1792]{1,0:T(8,128)(2,1)S(1)} %get-tuple-element.51), channel_id=1, source_target_pairs={{0,14},{2,0},{4,2},{6,4},{8,6},{10,8},{12,10},{14,12},{1,15},{3,1}... | collective-permute-start | bytes 258056 | tf_op jit(solution)/shard_map/spread/ppermute | solution.py:25
  (21 other events, 151.3 us)
where the time goes:
time: 203 us; the launch traced here: 202 us
  waiting for transfers between devices  105 us (52%)
  starting transfers between devices  65.4 us (32%)
  Pallas kernels  23.5 us (12%)
  other arithmetic  5.56 us (3%)
  local copies, waits for them, and re-layouts  2.3 us (1%)
    ppermute x26, waiting for transfers between devices, shift(): lax.ppermute(value, axis, [(i, (i + steps) % count) for i in range(count)])  69.6 us
    ppermute x26, starting transfers between devices, shift(): lax.ppermute(value, axis, [(i, (i + steps) % count) for i in range(count)])  40.5 us
    ppermute x6, waiting for transfers between devices, flip_x(): return lax.ppermute(value, X, [(i, i ^ bits) for i in range(NXH * NXL)])  32.4 us
    ppermute x4, starting transfers between devices, flip_core(): return lax.ppermute(value, 'core', [(0, 1), (1, 0)])  11.8 us
    pallas_call x2, Pallas kernels, gamma_of(): pl.pallas_call(functools.partial(gamma_kernel, group=group), out_shape=[j...  11.4 us
    pallas_call x1, Pallas kernels, on_device(): pl.pallas_call(coulomb_kernel, out_shape=[jax.ShapeDtypeStruct((NZ, rows,...  10.2 us
    ppermute x6, starting transfers between devices, flip_x(): return lax.ppermute(value, X, [(i, i ^ bits) for i in range(NXH * NXL)])  9.17 us
  transfers between devices with their start and end apart: 38, of which 25 were waited for; matrix products, arithmetic and copies ran while one was open for 1% of the time, Pallas kernels for 3%

commit v1 on v0

--- a/solution.py
+++ b/solution.py
@@ -13,6 +13,7 @@
 SH = ("z", "xl")
 X = ("xh", "xl")
 BF = jnp.bfloat16
+COLUMNS = (0, 1, 3, 2)
 F32 = jnp.float32
 
 
@@ -34,9 +35,18 @@
 
 
 def coulomb_kernel(own, xlf, bof, xh, *refs):
-    near, far, (out, send_up, send_down, stack, left) = refs[0:4], refs[4:8], refs[8:13]
+    near, far, (p0, p1, p2, p3, p5, p6, p7), refs = refs[0:3], refs[3:6], refs[6:13], refs[13:]
+    send_up, send_down, keep_up, keep_down, stack_out, out, stack, left, sem = refs
     z, xl, c = lax.axis_index("z"), lax.axis_index("xl"), lax.axis_index("core")
     rows, half = own.shape
+
+    for k, pieces in enumerate((near, far)):
+        at = 0
+        for piece in pieces:
+            stack[at:at + piece.shape[0], k * half:(k + 1) * half] = piece[...]
+            at += piece.shape[0]
+    copy = pltpu.make_async_copy(stack, stack_out, sem)
+    copy.start()
 
     def lay(mine, flipped, at):
         here, there = slice(at * half, (at + 1) * half), slice((1 - at) * half, (2 - at) * half)
@@ -53,17 +63,19 @@
     def _():
         lay(own, xlf, 1)
 
-    for d in range(NY):
-        for k, pieces in enumerate((near, far)):
-            stack[d * rows:(d + 1) * rows, k * half:(k + 1) * half] = pieces[d][...]
     for pair in range(NY // 2):
         got = dot_t(left[...], stack[pair * 2 * rows:(pair + 1) * 2 * rows, :])
         for e in range(2):
             for dd in range(2):
                 at = lax.rem(e * NY + pair * 2 + dd + NZ - z, NZ)
                 out[at] = got[e * rows:(e + 1) * rows, dd * rows:(dd + 1) * rows]
-    send_up[...] = out[NZ // 2, 0:rows // 2, :].astype(BF)
-    send_down[...] = out[NZ // 2, rows // 2:rows, :].astype(BF)
+    low, high = slice(0, rows // 2), slice(rows // 2, rows)
+    for k, ref in ((0, p0), (1, p1), (2, p2), (6, p6), (7, p7)):
+        ref[...] = out[k]
+    p3[...], p5[...] = out[3, low, :], out[5, high, :]
+    send_up[...], send_down[...] = out[4, low, :].astype(BF), out[4, high, :].astype(BF)
+    keep_up[...], keep_down[...] = out[3, high, :].astype(BF), out[5, low, :].astype(BF)
+    copy.wait()
 
 
 def combined_kernel(occ_ref, v_col, v_row, mine, up, down, out, scr):
@@ -72,7 +84,8 @@
     count = mine.shape[0] // virt
     e, d = z // NY, lax.rem(z, NY)
     row_occ = ((y * NXH + lax.rem(xh + e, NXH)) * NC + c) * count
-    col_occ = ((lax.rem(y + NY - d, NY) * NXH + xh) * NC + xl) * count
+    back = jnp.where(d < 2, d, NY + 1 - d)
+    col_occ = ((lax.rem(y + NY - back, NY) * NXH + xh) * NC + xl) * count
     for i in range(count):
         for j in range(count):
             tile = (pl.ds(i * virt, virt), pl.ds(j * virt, virt))
@@ -140,42 +153,51 @@
     with jax.named_scope("gather"):
         j0 = lax.ppermute(own, ("core", "xl"), [(0, 0), (1, 2), (2, 1), (3, 3)])
         bof = flip_x(own, 3)
-        xh = flip_x(own, 2)
+        xlf = lax.ppermute(own, ("core", "xl"), [(0, 1), (3, 2)])
+        j1, j3 = shift(j0, "y", 1), shift(j0, "y", -1)
         f0 = flip_core(j0)
-        j1, j2, j3 = (shift(j0, "y", d) for d in (1, 2, 3))
-        own_b, f0, bof, xh = lax.optimization_barrier((own, f0, bof, xh))
-        xlf = lax.ppermute(own_b, ("core", "xl"), [(0, 1), (3, 2)])
-        j1, j3, xlf = lax.optimization_barrier((j1, j3, xlf))
-        near = [j0, j1, j2, j3]
-        far = [f0] + [flip_core(p) for p in near[1:]]
+        own_b, f0, xlf = lax.optimization_barrier((own, f0, xlf))
+        xh = flip_x(own_b, 2)
+        j1, j3, bof = lax.optimization_barrier((j1, j3, bof))
+        j2a, j2b = shift(j1[:hr], "y", 1), shift(j3[hr:], "y", -1)
+        j2a, j2b, xh = lax.optimization_barrier((j2a, j2b, xh))
+        outer = jnp.concatenate([j1, j3])
+        outer_far = flip_core(outer)
+        inner = jnp.concatenate([j2a, j2b])
+        inner_far = flip_core(inner)
+        near, far = [j0, outer, inner], [f0, outer_far, inner_far]
 
     vmem = pl.BlockSpec(memory_space=pltpu.VMEM)
     smem = pl.BlockSpec(memory_space=pltpu.SMEM)
     params = pltpu.CompilerParams(vmem_limit_bytes=48 << 20)
 
     with jax.named_scope("coulomb"):
-        parts, up, down, stack = pl.pallas_call(
+        whole, part = jax.ShapeDtypeStruct((rows, rows), F32), jax.ShapeDtypeStruct((hr, rows), F32)
+        sent = jax.ShapeDtypeStruct((hr, rows), BF)
+        mine, p1, p2, p3, p5, p6, p7, up, down, keep_up, keep_down, stack = pl.pallas_call(
             coulomb_kernel,
-            out_shape=[
-                jax.ShapeDtypeStruct((NZ, rows, rows), F32),
-                jax.ShapeDtypeStruct((hr, rows), BF),
-                jax.ShapeDtypeStruct((hr, rows), BF),
-                jax.ShapeDtypeStruct((NY * rows, 2 * aux), BF),
+            out_shape=[whole, whole, whole, part, part, whole, whole, sent, sent, sent, sent]
+            + [jax.ShapeDtypeStruct((NY * rows, 2 * aux), BF)],
+            in_specs=[vmem] * 10,
+            out_specs=[vmem] * 11 + [pl.BlockSpec(memory_space=pl.ANY)],
+            scratch_shapes=[
+                pltpu.VMEM((NZ, rows, rows), F32),
+                pltpu.VMEM((NY * rows, 2 * aux), BF),
+                pltpu.VMEM((2 * rows, 2 * aux), BF),
+                pltpu.SemaphoreType.DMA,
             ],
-            in_specs=[vmem] * 12,
-            out_specs=[vmem] * 4,
-            scratch_shapes=[pltpu.VMEM((2 * rows, 2 * aux), BF)],
             compiler_params=params,
         )(own, xlf, bof, xh, *near, *far)
 
     with jax.named_scope("ring"):
         up, down = shift(up, "z", 1), shift(down, "z", -1)
-        up = jnp.concatenate([up.astype(F32) + parts[3, :hr], parts[3, hr:]])
-        down = jnp.concatenate([parts[5, :hr], down.astype(F32) + parts[5, hr:]])
-        for k in (2, 1, 0):
-            up, down = shift(up.astype(BF), "z", 1), shift(down.astype(BF), "z", -1)
-            if k:
-                up, down = up.astype(F32) + parts[k], down.astype(F32) + parts[NZ - k]
+        up = jnp.concatenate([(up.astype(F32) + p3).astype(BF), keep_up])
+        down = jnp.concatenate([keep_down, (down.astype(F32) + p5).astype(BF)])
+        for from_up, from_down in ((p2, p6), (p1, p7), (None, None)):
+            up, down = shift(up, "z", 1), shift(down, "z", -1)
+            if from_up is not None:
+                up = (up.astype(F32) + from_up).astype(BF)
+                down = (down.astype(F32) + from_down).astype(BF)
 
     with jax.named_scope("combined"):
         comb = pl.pallas_call(
@@ -185,7 +207,7 @@
             out_specs=vmem,
             scratch_shapes=[pltpu.VMEM((NXL, hr, rows), F32)],
             compiler_params=params,
-        )(occ_energy, virt_energy[:, None], virt_energy[None, :], parts[0], up, down)
+        )(occ_energy, virt_energy[:, None], virt_energy[None, :], mine, up, down)
         up1, down1 = shift(comb, "z", 1), shift(comb, "z", -1)
         up2, down2 = shift(up1, "z", 1), shift(down1, "z", -1)
         up3, down3 = shift(up2, "z", 1), shift(down2, "z", -1)
@@ -213,9 +235,9 @@
         mine0, mine1, to_xl0, to_xl1 = gamma_of(0, (F32, F32, F32, F32))
         to_both = jnp.concatenate([to_both0, to_both1 + via_xl.astype(F32)]).astype(BF)
         to_xl = jnp.concatenate([to_xl0 + via_both.astype(F32), to_xl1]).astype(BF)
-        mine = jnp.concatenate([mine0, mine1])
+        kept = jnp.concatenate([mine0, mine1])
         from_both, from_xl = flip_x(to_both, 3), flip_x(to_xl, 1)
-        total = (mine + from_xl.astype(F32) + from_both.astype(F32)).astype(BF)
+        total = (kept + from_xl.astype(F32) + from_both.astype(F32)).astype(BF)
 
     with jax.named_scope("spread"):
         got = [total[0]] + [shift(total[k], "z", k) for k in range(1, NZ)]

time: 203 us -> 191 us (0.941)
  waiting for transfers between devices: 105 us -> 90.5 us
  starting transfers between devices: 65.4 us -> 72.6 us
  other arithmetic: 5.56 us -> 2.73 us
    ppermute x4 -> x3, starting transfers between devices: 11.8 us -> 0.28 us  [flip_core(): return lax.ppermute(value, 'core', [(0, 1), (1, 0)])]
    ppermute x26 -> x27, waiting for transfers between devices: 69.6 us -> 59.2 us  [shift(): lax.ppermute(value, axis, [(i, (i + steps) % count) for i in range(count)])]
    ppermute x6, waiting for transfers between devices: 32.4 us -> 22.4 us  [flip_x(): return lax.ppermute(value, X, [(i, i ^ bits) for i in range(NXH * NXL)])]
    ppermute x26 -> x27, starting transfers between devices: 40.5 us -> 48.4 us  [shift(): lax.ppermute(value, axis, [(i, (i + steps) % count) for i in range(count)])]
    ppermute x1, starting transfers between devices: 3.19 us -> 10.6 us  [on_device(): xlf = lax.ppermute(own, ('core', 'xl'), [(0, 1), (3, 2)])]
    ppermute x1, waiting for transfers between devices: 0.01 us -> 6.82 us  [on_device(): xlf = lax.ppermute(own, ('core', 'xl'), [(0, 1), (3, 2)])]
    ppermute x6, starting transfers between devices: 9.17 us -> 12.6 us  [flip_x(): return lax.ppermute(value, X, [(i, i ^ bits) for i in range(NXH * NXL)])]
    another operation x6 -> x4, other arithmetic: 3.03 us -> 0.19 us
  transfers between devices with their start and end apart: 38 -> 38, of which waited for: 25 -> 23; matrix products, arithmetic and copies ran while one was open for 1% -> 1% of each run, Pallas kernels for 3% -> 3%
where the time goes in v1:
time: 191 us
  waiting for transfers between devices  90.5 us (47%)
  starting transfers between devices  72.6 us (38%)
  Pallas kernels  21.6 us (11%)
  other arithmetic  2.73 us (1%)
  local copies, waits for them, and re-layouts  2.62 us (1%)
    ppermute x27, waiting for transfers between devices, shift(): lax.ppermute(value, axis, [(i, (i + steps) % count) for i in range(count)])  59.2 us
    ppermute x27, starting transfers between devices, shift(): lax.ppermute(value, axis, [(i, (i + steps) % count) for i in range(count)])  48.4 us
    ppermute x6, waiting for transfers between devices, flip_x(): return lax.ppermute(value, X, [(i, i ^ bits) for i in range(NXH * NXL)])  22.4 us
    ppermute x6, starting transfers between devices, flip_x(): return lax.ppermute(value, X, [(i, i ^ bits) for i in range(NXH * NXL)])  12.6 us
    pallas_call x2, Pallas kernels, gamma_of(): pl.pallas_call(functools.partial(gamma_kernel, group=group), out_shape=[j...  11.4 us
    ppermute x1, starting transfers between devices, on_device(): xlf = lax.ppermute(own, ('core', 'xl'), [(0, 1), (3, 2)])  10.6 us
    pallas_call x1, Pallas kernels, on_device(): pl.pallas_call(coulomb_kernel, out_shape=[whole, whole, whole, part, part...  8.3 us
    ppermute x1, waiting for transfers between devices, on_device(): xlf = lax.ppermute(own, ('core', 'xl'), [(0, 1), (3, 2)])  6.82 us
  transfers between devices with their start and end apart: 38, of which 23 were waited for; matrix products, arithmetic and copies ran while one was open for 1% of the time, Pallas kernels for 3%

profile of v1, /device:TPU:32, one launch (start us, length us, event | category | flops | bytes accessed | tf_op | source)
XLA Modules:
  0.0 190.5 jit_solution(17303961625494354822)
XLA Ops:
  2.7 4.3 %collective-permute-start.5 = (bf16[384,896]{1,0:T(8,128)(2,1)S(1)}, bf16[384,896]{1,0:T(8,128)(2,1)S(1)}, u32[]{:S(2)}, u32[]{:S(2)}) collective-permute-start(bf16[384,896]{1,0:T(8,128)(2,1)S(1)} %bitcast.29), channel_id=1, source_target_pairs={{0,33},{1,32},{32,1},{33,0},{2,35},{3,34},{34,3},{35,2},{4,37},{5,... | collective-permute-start | bytes 2064392 | tf_op jit(solution)/shard_map/gather/ppermute | solution.py:21
  10.2 10.6 %collective-permute-start.2 = (bf16[384,896]{1,0:T(8,128)(2,1)S(1)}, bf16[384,896]{1,0:T(8,128)(2,1)S(1)}, u32[]{:S(2)}, u32[]{:S(2)}) collective-permute-start(bf16[384,896]{1,0:T(8,128)(2,1)S(1)} %bitcast.30), channel_id=1, source_target_pairs={{0,1},{17,16},{2,3},{19,18},{4,5},{21,20},{6,7},{23,22},{8,9},{25,... | collective-permute-start | bytes 2064392 | tf_op jit(solution)/shard_map/gather/ppermute | solution.py:156
  22.5 6.8 %collective-permute-done.2.xlf = bf16[384,896]{1,0:T(8,128)(2,1)S(1)} collective-permute-done((bf16[384,896]{1,0:T(8,128)(2,1)S(1)}, bf16[384,896]{1,0:T(8,128)(2,1)S(1)}, u32[]{:S(2)}, u32[]{:S(2)}) %collective-permute-start.2) | collective-permute-done | bytes 688160 | tf_op jit(solution)/shard_map/gather/ppermute | solution.py:156
  35.7 8.4 %collective-permute-done.6 = bf16[192,896]{1,0:T(8,128)(2,1)S(1)} collective-permute-done((bf16[192,896]{1,0:T(8,128)(2,1)S(1)}, bf16[192,896]{1,0:T(8,128)(2,1)S(1)}, u32[]{:S(2)}, u32[]{:S(2)}) %collective-permute-start.6) | collective-permute-done | bytes 344096 | tf_op jit(solution)/shard_map/gather/ppermute | solution.py:26
  44.1 3.5 %collective-permute-done.8.xh = bf16[384,896]{1,0:T(8,128)(2,1)S(1)} collective-permute-done((bf16[384,896]{1,0:T(8,128)(2,1)S(1)}, bf16[384,896]{1,0:T(8,128)(2,1)S(1)}, u32[]{:S(2)}, u32[]{:S(2)}) %collective-permute-start.8) | collective-permute-done | bytes 688160 | tf_op jit(solution)/shard_map/gather/ppermute | solution.py:21
  52.0 8.3 %coulomb.1 = (f32[384,384]{1,0:T(8,128)S(1)}, f32[384,384]{1,0:T(8,128)S(1)}, f32[384,384]{1,0:T(8,128)S(1)}, f32[192,384]{1,0:T(8,128)S(1)}, f32[192,384]{1,0:T...) custom-call(bf16[384,896]{1,0:T(8,128)(2,1)S(1)} %bitcast.32, ...), custom_call_target="tpu_custom_call" | custom-call | tf_op jit(solution)/shard_map/coulomb/pallas_call | solution.py:177
  62.4 4.0 %collective-permute-done.15 = bf16[192,384]{1,0:T(8,128)(2,1)S(1)} collective-permute-done((bf16[192,384]{1,0:T(8,128)(2,1)S(1)}, bf16[192,384]{1,0:T(8,128)(2,1)S(1)}, u32[]{:S(2)}, u32[]{:S(2)}) %collective-permute-start.15) | collective-permute-done | bytes 147488 | tf_op jit(solution)/shard_map/ring/ppermute | solution.py:26
  66.5 3.6 %collective-permute-start.16 = (bf16[384,384]{1,0:T(8,128)(2,1)S(1)}, bf16[384,384]{1,0:T(8,128)(2,1)S(1)}, u32[]{:S(2)}, u32[]{:S(2)}) collective-permute-start(bf16[384,384]{1,0:T(8,128)(2,1)S(1)} %pad_maximum_fusion.3), channel_id=1, source_target_pairs={{0,14},{2,0},{4,2},{6,4},{8,6},{10,8},{12,10},{14,12},{1,15},{3,1}... | collective-permute-start | bytes 884744 | tf_op jit(solution)/shard_map/ring/ppermute | solution.py:26
  70.4 5.4 %collective-permute-done.16 = bf16[384,384]{1,0:T(8,128)(2,1)S(1)} collective-permute-done((bf16[384,384]{1,0:T(8,128)(2,1)S(1)}, bf16[384,384]{1,0:T(8,128)(2,1)S(1)}, u32[]{:S(2)}, u32[]{:S(2)}) %collective-permute-start.16) | collective-permute-done | bytes 294944 | tf_op jit(solution)/shard_map/ring/ppermute | solution.py:26
  75.9 3.8 %collective-permute-start.17 = (bf16[384,384]{1,0:T(8,128)(2,1)S(1)}, bf16[384,384]{1,0:T(8,128)(2,1)S(1)}, u32[]{:S(2)}, u32[]{:S(2)}) collective-permute-start(bf16[384,384]{1,0:T(8,128)(2,1)S(1)} %add_convert_fusion.3), channel_id=1, source_target_pairs={{0,14},{2,0},{4,2},{6,4},{8,6},{10,8},{12,10},{14,12},{1,15},{3,1}... | collective-permute-start | bytes 884744 | tf_op jit(solution)/shard_map/ring/ppermute | solution.py:26
  80.3 4.4 %collective-permute-done.17 = bf16[384,384]{1,0:T(8,128)(2,1)S(1)} collective-permute-done((bf16[384,384]{1,0:T(8,128)(2,1)S(1)}, bf16[384,384]{1,0:T(8,128)(2,1)S(1)}, u32[]{:S(2)}, u32[]{:S(2)}) %collective-permute-start.17) | collective-permute-done | bytes 294944 | tf_op jit(solution)/shard_map/ring/ppermute | solution.py:26
  89.1 3.6 %collective-permute-done.18.down = bf16[384,384]{1,0:T(8,128)(2,1)S(1)} collective-permute-done((bf16[384,384]{1,0:T(8,128)(2,1)S(1)}, bf16[384,384]{1,0:T(8,128)(2,1)S(1)}, u32[]{:S(2)}, u32[]{:S(2)}) %collective-permute-start.18) | collective-permute-done | bytes 294944 | tf_op jit(solution)/shard_map/ring/ppermute | solution.py:26
  92.6 4.2 %collective-permute-done.14.up = bf16[384,384]{1,0:T(8,128)(2,1)S(1)} collective-permute-done((bf16[384,384]{1,0:T(8,128)(2,1)S(1)}, bf16[384,384]{1,0:T(8,128)(2,1)S(1)}, u32[]{:S(2)}, u32[]{:S(2)}) %collective-permute-start.14) | collective-permute-done | bytes 294944 | tf_op jit(solution)/shard_map/ring/ppermute | solution.py:26
  101.3 5.6 %collective-permute-done.19.refs_1_ = bf16[2,192,384]{2,1,0:T(8,128)(2,1)S(1)} collective-permute-done((bf16[2,192,384]{2,1,0:T(8,128)(2,1)S(1)}, bf16[2,192,384]{2,1,0:T(8,128)(2,1)S(1)}, u32[]{:S(2)}, u32[]{:S(2)}) %collective-permute-start.19) | collective-permute-done | bytes 294944 | tf_op jit(solution)/shard_map/combined/ppermute | solution.py:26
  110.4 6.8 %collective-permute-done.21.refs_3_ = bf16[2,192,384]{2,1,0:T(8,128)(2,1)S(1)} collective-permute-done((bf16[2,192,384]{2,1,0:T(8,128)(2,1)S(1)}, bf16[2,192,384]{2,1,0:T(8,128)(2,1)S(1)}, u32[]{:S(2)}, u32[]{:S(2)}) %collective-permute-start.21) | collective-permute-done | bytes 294944 | tf_op jit(solution)/shard_map/combined/ppermute | solution.py:26
  117.2 3.7 %collective-permute-start.24 = (bf16[2,192,384]{2,1,0:T(8,128)(2,1)S(1)}, bf16[2,192,384]{2,1,0:T(8,128)(2,1)S(1)}, u32[]{:S(2)}, u32[]{:S(2)}) collective-permute-start(bf16[2,192,384]{2,1,0:T(8,128)(2,1)S(1)} %collective-permute-done.22.refs_4_), channel_id=1, source_target_pairs={{0,14},{2,0},{4,2},{6,4},{8,6},{10,8},{12,10},{14,12},{1,15},{3,1}... | collective-permute-start | bytes 884744 | tf_op jit(solution)/shard_map/combined/ppermute | solution.py:26
  120.9 6.1 %collective-permute-done.23.refs_5_ = bf16[2,192,384]{2,1,0:T(8,128)(2,1)S(1)} collective-permute-done((bf16[2,192,384]{2,1,0:T(8,128)(2,1)S(1)}, bf16[2,192,384]{2,1,0:T(8,128)(2,1)S(1)}, u32[]{:S(2)}, u32[]{:S(2)}) %collective-permute-start.23) | collective-permute-done | bytes 294944 | tf_op jit(solution)/shard_map/combined/ppermute | solution.py:26
  133.2 5.8 %gamma.3 = (bf16[4,24,1792]{2,1,0:T(8,128)(2,1)S(1)}, bf16[4,24,1792]{2,1,0:T(8,128)(2,1)S(1)}, f32[4,24,1792]{2,1,0:T(8,128)S(1)}, f32[4,24,1792]{2,1,0:T(8,128)S(1)}) custom-call(bf16[2,192,384]{2,1,0:T(8,128)(2,1)S(1)} %combined.1.refs_0_, bf16[2,192,384]{2,1,0:T(8,128)(2,1)S(1)} %collective-permute-done.19.refs_1_, ...), custom_call_target="tpu_custom_call" | custom-call | tf_op jit(solution)/shard_map/gamma/pallas_call | solution.py:221
  140.4 5.6 %gamma.2 = (f32[4,24,1792]{2,1,0:T(8,128)S(1)}, f32[4,24,1792]{2,1,0:T(8,128)S(1)}, f32[4,24,1792]{2,1,0:T(8,128)S(1)}, f32[4,24,1792]{2,1,0:T(8,128)S(1)}) custom-call(bf16[2,192,384]{2,1,0:T(8,128)(2,1)S(1)} %combined.1.refs_0_, bf16[2,192,384]{2,1,0:T(8,128)(2,1)S(1)} %collective-permute-done.19.refs_1_, ...), custom_call_target="tpu_custom_call" | custom-call | tf_op jit(solution)/shard_map/gamma/pallas_call | solution.py:221
  148.5 7.1 %collective-permute-done.29 = bf16[4,24,1792]{2,1,0:T(8,128)(2,1)S(1)} collective-permute-done((bf16[4,24,1792]{2,1,0:T(8,128)(2,1)S(1)}, bf16[4,24,1792]{2,1,0:T(8,128)(2,1)S(1)}, u32[]{:S(2)}, u32[]{:S(2)}) %collective-permute-start.29) | collective-permute-done | bytes 344096 | tf_op jit(solution)/shard_map/gamma/ppermute | solution.py:21
  157.6 5.3 %collective-permute-done.28 = bf16[8,24,1792]{2,1,0:T(8,128)(2,1)S(1)} collective-permute-done((bf16[8,24,1792]{2,1,0:T(8,128)(2,1)S(1)}, bf16[8,24,1792]{2,1,0:T(8,128)(2,1)S(1)}, u32[]{:S(2)}, u32[]{:S(2)}) %collective-permute-start.28) | collective-permute-done | bytes 688160 | tf_op jit(solution)/shard_map/gamma/ppermute | solution.py:21
  162.9 5.0 %collective-permute-done.30 = bf16[8,24,1792]{2,1,0:T(8,128)(2,1)S(1)} collective-permute-done((bf16[8,24,1792]{2,1,0:T(8,128)(2,1)S(1)}, bf16[8,24,1792]{2,1,0:T(8,128)(2,1)S(1)}, u32[]{:S(2)}, u32[]{:S(2)}) %collective-permute-start.30) | collective-permute-done | bytes 688160 | tf_op jit(solution)/shard_map/gamma/ppermute | solution.py:21
  172.2 4.3 %collective-permute-start.33 = (bf16[24,1792]{1,0:T(8,128)(2,1)S(1)}, bf16[24,1792]{1,0:T(8,128)(2,1)S(1)}, u32[]{:S(2)}, u32[]{:S(2)}) collective-permute-start(bf16[24,1792]{1,0:T(8,128)(2,1)S(1)} %get-tuple-element.67), channel_id=1, source_target_pairs={{0,6},{2,8},{4,10},{6,12},{8,14},{10,0},{12,2},{14,4},{1,7},{3,9},... | collective-permute-start | bytes 258056 | tf_op jit(solution)/shard_map/spread/ppermute | solution.py:26
  183.2 3.8 %collective-permute-done.34.refs_4_ = bf16[24,1792]{1,0:T(8,128)(2,1)S(1)} collective-permute-done((bf16[24,1792]{1,0:T(8,128)(2,1)S(1)}, bf16[24,1792]{1,0:T(8,128)(2,1)S(1)}, u32[]{:S(2)}, u32[]{:S(2)}) %collective-permute-start.34) | collective-permute-done | bytes 86048 | tf_op jit(solution)/shard_map/spread/ppermute | solution.py:26
  (105 shorter events, 60.0 us)
Async XLA Ops:
  2.7 19.8 %collective-permute-start.5 = (bf16[384,896]{1,0:T(8,128)(2,1)S(1)}, bf16[384,896]{1,0:T(8,128)(2,1)S(1)}, u32[]{:S(2)}, u32[]{:S(2)}) collective-permute-start(bf16[384,896]{1,0:T(8,128)(2,1)S(1)} %bitcast.29), channel_id=1, source_target_pairs={{0,33},{1,32},{32,1},{33,0},{2,35},{3,34},{34,3},{35,2},{4,37},{5,... | collective-permute-start | bytes 2064392 | tf_op jit(solution)/shard_map/gather/ppermute | solution.py:21
  7.0 15.5 %collective-permute-start.3 = (bf16[384,896]{1,0:T(8,128)(2,1)S(1)}, bf16[384,896]{1,0:T(8,128)(2,1)S(1)}, u32[]{:S(2)}, u32[]{:S(2)}) collective-permute-start(bf16[384,896]{1,0:T(8,128)(2,1)S(1)} %collective-permute-done.refs_0_), channel_id=1, source_target_pairs={{0,64},{64,128},{128,192},{192,0},{1,65},{65,129},{129,193},{193,1... | collective-permute-start | bytes 2064392 | tf_op jit(solution)/shard_map/gather/ppermute | solution.py:26
  8.6 13.9 %collective-permute-start.4 = (bf16[384,896]{1,0:T(8,128)(2,1)S(1)}, bf16[384,896]{1,0:T(8,128)(2,1)S(1)}, u32[]{:S(2)}, u32[]{:S(2)}) collective-permute-start(bf16[384,896]{1,0:T(8,128)(2,1)S(1)} %collective-permute-done.refs_0_), channel_id=1, source_target_pairs={{0,192},{64,0},{128,64},{192,128},{1,193},{65,1},{129,65},{193,129... | collective-permute-start | bytes 2064392 | tf_op jit(solution)/shard_map/gather/ppermute | solution.py:26
  10.2 19.1 %collective-permute-start.2 = (bf16[384,896]{1,0:T(8,128)(2,1)S(1)}, bf16[384,896]{1,0:T(8,128)(2,1)S(1)}, u32[]{:S(2)}, u32[]{:S(2)}) collective-permute-start(bf16[384,896]{1,0:T(8,128)(2,1)S(1)} %bitcast.30), channel_id=1, source_target_pairs={{0,1},{17,16},{2,3},{19,18},{4,5},{21,20},{6,7},{23,22},{8,9},{25,... | collective-permute-start | bytes 2064392 | tf_op jit(solution)/shard_map/gather/ppermute | solution.py:156
  29.3 18.4 %collective-permute-start.8 = (bf16[384,896]{1,0:T(8,128)(2,1)S(1)}, bf16[384,896]{1,0:T(8,128)(2,1)S(1)}, u32[]{:S(2)}, u32[]{:S(2)}) collective-permute-start(bf16[384,896]{1,0:T(8,128)(2,1)S(1)} %bitcast.31), channel_id=1, source_target_pairs={{0,32},{1,33},{32,0},{33,1},{2,34},{3,35},{34,2},{35,3},{4,36},{5,... | collective-permute-start | bytes 2064392 | tf_op jit(solution)/shard_map/gather/ppermute | solution.py:21
  32.2 17.8 %collective-permute-start.9 = (bf16[768,896]{1,0:T(8,128)(2,1)S(1)}, bf16[768,896]{1,0:T(8,128)(2,1)S(1)}, u32[]{:S(2)}, u32[]{:S(2)}) collective-permute-start(bf16[768,896]{1,0:T(8,128)(2,1)S(1)} %constant_dynamic-update-slice_fusion.refs_1_), channel_id=1, source_target_pairs={{0,16},{16,0},{1,17},{17,1},{2,18},{18,2},{3,19},{19,3},{4,20},{20... | collective-permute-start | bytes 4128776 | tf_op jit(solution)/shard_map/gather/ppermute | solution.py:30
  32.4 11.7 %collective-permute-start.6 = (bf16[192,896]{1,0:T(8,128)(2,1)S(1)}, bf16[192,896]{1,0:T(8,128)(2,1)S(1)}, u32[]{:S(2)}, u32[]{:S(2)}) collective-permute-start(bf16[192,896]{1,0:T(8,128)(2,1)S(1)} %slice.36), channel_id=1, source_target_pairs={{0,64},{64,128},{128,192},{192,0},{1,65},{65,129},{129,193},{193,1... | collective-permute-start | bytes 1032200 | tf_op jit(solution)/shard_map/gather/ppermute | solution.py:26
  32.8 11.3 %collective-permute-start.7 = (bf16[192,896]{1,0:T(8,128)(2,1)S(1)}, bf16[192,896]{1,0:T(8,128)(2,1)S(1)}, u32[]{:S(2)}, u32[]{:S(2)}) collective-permute-start(bf16[192,896]{1,0:T(8,128)(2,1)S(1)} %slice.37), channel_id=1, source_target_pairs={{0,192},{64,0},{128,64},{192,128},{1,193},{65,1},{129,65},{193,129... | collective-permute-start | bytes 1032200 | tf_op jit(solution)/shard_map/gather/ppermute | solution.py:26
  60.5 9.7 %collective-permute-start.11 = (bf16[192,384]{1,0:T(8,128)(2,1)S(1)}, bf16[192,384]{1,0:T(8,128)(2,1)S(1)}, u32[]{:S(2)}, u32[]{:S(2)}) collective-permute-start(bf16[192,384]{1,0:T(8,128)(2,1)S(1)} %get-tuple-element.44), channel_id=1, source_target_pairs={{0,2},{2,4},{4,6},{6,8},{8,10},{10,12},{12,14},{14,0},{1,3},{3,5},... | collective-permute-start | bytes 442376 | tf_op jit(solution)/shard_map/ring/ppermute | solution.py:26
  66.5 9.3 %collective-permute-start.16 = (bf16[384,384]{1,0:T(8,128)(2,1)S(1)}, bf16[384,384]{1,0:T(8,128)(2,1)S(1)}, u32[]{:S(2)}, u32[]{:S(2)}) collective-permute-start(bf16[384,384]{1,0:T(8,128)(2,1)S(1)} %pad_maximum_fusion.3), channel_id=1, source_target_pairs={{0,14},{2,0},{4,2},{6,4},{8,6},{10,8},{12,10},{14,12},{1,15},{3,1}... | collective-permute-start | bytes 884744 | tf_op jit(solution)/shard_map/ring/ppermute | solution.py:26
  70.3 9.8 %collective-permute-start.12 = (bf16[384,384]{1,0:T(8,128)(2,1)S(1)}, bf16[384,384]{1,0:T(8,128)(2,1)S(1)}, u32[]{:S(2)}, u32[]{:S(2)}) collective-permute-start(bf16[384,384]{1,0:T(8,128)(2,1)S(1)} %pad_maximum_fusion.2), channel_id=1, source_target_pairs={{0,2},{2,4},{4,6},{6,8},{8,10},{10,12},{12,14},{14,0},{1,3},{3,5},... | collective-permute-start | bytes 884744 | tf_op jit(solution)/shard_map/ring/ppermute | solution.py:26
  97.9 9.0 %collective-permute-start.19 = (bf16[2,192,384]{2,1,0:T(8,128)(2,1)S(1)}, bf16[2,192,384]{2,1,0:T(8,128)(2,1)S(1)}, u32[]{:S(2)}, u32[]{:S(2)}) collective-permute-start(bf16[2,192,384]{2,1,0:T(8,128)(2,1)S(1)} %combined.1.refs_0_), channel_id=1, source_target_pairs={{0,2},{2,4},{4,6},{6,8},{8,10},{10,12},{12,14},{14,0},{1,3},{3,5},... | collective-permute-start | bytes 884744 | tf_op jit(solution)/shard_map/combined/ppermute | solution.py:26
  106.9 10.3 %collective-permute-start.21 = (bf16[2,192,384]{2,1,0:T(8,128)(2,1)S(1)}, bf16[2,192,384]{2,1,0:T(8,128)(2,1)S(1)}, u32[]{:S(2)}, u32[]{:S(2)}) collective-permute-start(bf16[2,192,384]{2,1,0:T(8,128)(2,1)S(1)} %collective-permute-done.19.refs_1_), channel_id=1, source_target_pairs={{0,2},{2,4},{4,6},{6,8},{8,10},{10,12},{12,14},{14,0},{1,3},{3,5},... | collective-permute-start | bytes 884744 | tf_op jit(solution)/shard_map/combined/ppermute | solution.py:26
  106.9 10.3 %collective-permute-start.22 = (bf16[2,192,384]{2,1,0:T(8,128)(2,1)S(1)}, bf16[2,192,384]{2,1,0:T(8,128)(2,1)S(1)}, u32[]{:S(2)}, u32[]{:S(2)}) collective-permute-start(bf16[2,192,384]{2,1,0:T(8,128)(2,1)S(1)} %collective-permute-done.20.refs_2_), channel_id=1, source_target_pairs={{0,14},{2,0},{4,2},{6,4},{8,6},{10,8},{12,10},{14,12},{1,15},{3,1}... | collective-permute-start | bytes 884744 | tf_op jit(solution)/shard_map/combined/ppermute | solution.py:26
  117.2 9.8 %collective-permute-start.23 = (bf16[2,192,384]{2,1,0:T(8,128)(2,1)S(1)}, bf16[2,192,384]{2,1,0:T(8,128)(2,1)S(1)}, u32[]{:S(2)}, u32[]{:S(2)}) collective-permute-start(bf16[2,192,384]{2,1,0:T(8,128)(2,1)S(1)} %collective-permute-done.21.refs_3_), channel_id=1, source_target_pairs={{0,2},{2,4},{4,6},{6,8},{8,10},{10,12},{12,14},{14,0},{1,3},{3,5},... | collective-permute-start | bytes 884744 | tf_op jit(solution)/shard_map/combined/ppermute | solution.py:26
  117.2 9.9 %collective-permute-start.24 = (bf16[2,192,384]{2,1,0:T(8,128)(2,1)S(1)}, bf16[2,192,384]{2,1,0:T(8,128)(2,1)S(1)}, u32[]{:S(2)}, u32[]{:S(2)}) collective-permute-start(bf16[2,192,384]{2,1,0:T(8,128)(2,1)S(1)} %collective-permute-done.22.refs_4_), channel_id=1, source_target_pairs={{0,14},{2,0},{4,2},{6,4},{8,6},{10,8},{12,10},{14,12},{1,15},{3,1}... | collective-permute-start | bytes 884744 | tf_op jit(solution)/shard_map/combined/ppermute | solution.py:26
  146.1 9.5 %collective-permute-start.29 = (bf16[4,24,1792]{2,1,0:T(8,128)(2,1)S(1)}, bf16[4,24,1792]{2,1,0:T(8,128)(2,1)S(1)}, u32[]{:S(2)}, u32[]{:S(2)}) collective-permute-start(bf16[4,24,1792]{2,1,0:T(8,128)(2,1)S(1)} %get-tuple-element.62), channel_id=1, source_target_pairs={{0,1},{1,0},{32,33},{33,32},{2,3},{3,2},{34,35},{35,34},{4,5},{5,4... | collective-permute-start | bytes 1032200 | tf_op jit(solution)/shard_map/gamma/ppermute | solution.py:21
  147.9 15.0 %collective-permute-start.28 = (bf16[8,24,1792]{2,1,0:T(8,128)(2,1)S(1)}, bf16[8,24,1792]{2,1,0:T(8,128)(2,1)S(1)}, u32[]{:S(2)}, u32[]{:S(2)}) collective-permute-start(bf16[8,24,1792]{2,1,0:T(8,128)(2,1)S(1)} %pad_maximum_fusion), channel_id=1, source_target_pairs={{0,1},{1,0},{32,33},{33,32},{2,3},{3,2},{34,35},{35,34},{4,5},{5,4... | collective-permute-start | bytes 2064392 | tf_op jit(solution)/shard_map/gamma/ppermute | solution.py:21
  155.7 12.2 %collective-permute-start.30 = (bf16[8,24,1792]{2,1,0:T(8,128)(2,1)S(1)}, bf16[8,24,1792]{2,1,0:T(8,128)(2,1)S(1)}, u32[]{:S(2)}, u32[]{:S(2)}) collective-permute-start(bf16[8,24,1792]{2,1,0:T(8,128)(2,1)S(1)} %pad_maximum_fusion.1), channel_id=1, source_target_pairs={{0,33},{1,32},{32,1},{33,0},{2,35},{3,34},{34,3},{35,2},{4,37},{5,... | collective-permute-start | bytes 2064392 | tf_op jit(solution)/shard_map/gamma/ppermute | solution.py:21
  168.2 12.9 %collective-permute-start.31 = (bf16[24,1792]{1,0:T(8,128)(2,1)S(1)}, bf16[24,1792]{1,0:T(8,128)(2,1)S(1)}, u32[]{:S(2)}, u32[]{:S(2)}) collective-permute-start(bf16[24,1792]{1,0:T(8,128)(2,1)S(1)} %get-tuple-element.69), channel_id=1, source_target_pairs={{0,2},{2,4},{4,6},{6,8},{8,10},{10,12},{12,14},{14,0},{1,3},{3,5},... | collective-permute-start | bytes 258056 | tf_op jit(solution)/shard_map/spread/ppermute | solution.py:26
  169.9 11.9 %collective-permute-start.32 = (bf16[24,1792]{1,0:T(8,128)(2,1)S(1)}, bf16[24,1792]{1,0:T(8,128)(2,1)S(1)}, u32[]{:S(2)}, u32[]{:S(2)}) collective-permute-start(bf16[24,1792]{1,0:T(8,128)(2,1)S(1)} %get-tuple-element.68), channel_id=1, source_target_pairs={{0,4},{2,6},{4,8},{6,10},{8,12},{10,14},{12,0},{14,2},{1,5},{3,7},... | collective-permute-start | bytes 258056 | tf_op jit(solution)/shard_map/spread/ppermute | solution.py:26
  172.2 10.9 %collective-permute-start.33 = (bf16[24,1792]{1,0:T(8,128)(2,1)S(1)}, bf16[24,1792]{1,0:T(8,128)(2,1)S(1)}, u32[]{:S(2)}, u32[]{:S(2)}) collective-permute-start(bf16[24,1792]{1,0:T(8,128)(2,1)S(1)} %get-tuple-element.67), channel_id=1, source_target_pairs={{0,6},{2,8},{4,10},{6,12},{8,14},{10,0},{12,2},{14,4},{1,7},{3,9},... | collective-permute-start | bytes 258056 | tf_op jit(solution)/shard_map/spread/ppermute | solution.py:26
  176.6 10.4 %collective-permute-start.34 = (bf16[24,1792]{1,0:T(8,128)(2,1)S(1)}, bf16[24,1792]{1,0:T(8,128)(2,1)S(1)}, u32[]{:S(2)}, u32[]{:S(2)}) collective-permute-start(bf16[24,1792]{1,0:T(8,128)(2,1)S(1)} %get-tuple-element.66), channel_id=1, source_target_pairs={{0,8},{2,10},{4,12},{6,14},{8,0},{10,2},{12,4},{14,6},{1,9},{3,11}... | collective-permute-start | bytes 258056 | tf_op jit(solution)/shard_map/spread/ppermute | solution.py:26
  178.6 9.9 %collective-permute-start.35 = (bf16[24,1792]{1,0:T(8,128)(2,1)S(1)}, bf16[24,1792]{1,0:T(8,128)(2,1)S(1)}, u32[]{:S(2)}, u32[]{:S(2)}) collective-permute-start(bf16[24,1792]{1,0:T(8,128)(2,1)S(1)} %get-tuple-element.65), channel_id=1, source_target_pairs={{0,10},{2,12},{4,14},{6,0},{8,2},{10,4},{12,6},{14,8},{1,11},{3,13... | collective-permute-start | bytes 258056 | tf_op jit(solution)/shard_map/spread/ppermute | solution.py:26
  (23 other events, 176.9 us)
